TPU v7x, 32 devices: a whole 2x2x4 slice. The times are simulated.
32 devices in a mesh: row: 4 (over y, core), col: 8 (over z, x).
Axes of the slice: x: 2, y: 2, z: 4, core: 2. Of those that a mesh axis runs over, the one named last changes fastest.
Arguments:
- slip: bfloat16 [32, 128, 3, 256], P(('row', 'col')), may hold values from -6 to 6
- near_pairs: int32 [512, 2], P(('row', 'col')), may hold values from 0 to 7, as said below
- near_blocks: bfloat16 [512, 768, 768], P(('row', 'col')), may hold values from -0.0546875 to 0.0546875
- near_live: int32 [32], P(('row', 'col')), may hold values from 1 to 16, as said below
- far_pairs: int32 [512, 2], P(('row', 'col')), may hold values from 0 to 7, as said below
- far_left: bfloat16 [512, 768, 32], P(('row', 'col')), may hold values from -0.21875 to 0.21875
- far_right: bfloat16 [512, 768, 32], P(('row', 'col')), may hold values from -0.21875 to 0.21875
Outputs:
- traction: bfloat16 [32, 128, 3, 256], P(('row', 'col'))
- response: bfloat16 [32, 128, 3, 256], P(('row', 'col'))
Inputs may be any that keep to these rules, and one draw needn't show every extreme that they name: `near_pairs`: for a slot of group g, with a = g // 8, b = g % 8, first entry p and second entry q: p is below 8, q is below 4, and a * 8 + p <= q * 8 + b. `far_pairs`: the same rule as for the near-field pairs, with groups of 16 slots. `near_live`: some group has all 16 slots live.
All inputs are finite; a program needn't handle non-finite values.
Results may differ from a plain program's by a relative error of at most 0.022.
Values may be sent and summed in bfloat16 or wider, within the bound.
A program may use at most 192 MiB of HBM per device.

v0:
```python
import functools

import jax
import jax.numpy as jnp
from jax import lax
from jax.experimental import pallas as pl
from jax.experimental.pallas import tpu as pltpu
from jax.sharding import PartitionSpec as P

MESH = pl.DeviceIdType.MESH
TRANS_B = (((1,), (1,)), ((), ()))


def both_products(dims, plan, field, planes, lcat, rcat, blocks_hbm, traction, response,
                  blocks, rg0, rg1, cg0, cg1, rp, xr, zr, zs, cp, cr, yr, ys, runs,
                  blk_sem, rg_rs, cg_rs, z_ss, x_ss, cgy_ss, cgc_ss,
                  xr_ss, xr_rs, zr_ss, zr_rs, cr_ss, cr_rs, yr_ss, yr_rs):
    A, B, R, S, parts = dims
    NC, NR = A * B, 2 * R
    slips, width = field.shape
    a, b = lax.axis_index("row"), lax.axis_index("col")
    z, x = b // B, b % B
    y, c = a // 2, a % 2
    f32, bf16 = jnp.float32, jnp.bfloat16

    def rcopy(src, dst, ss, rs, dev):
        return pltpu.make_async_remote_copy(
            src_ref=src, dst_ref=dst, send_sem=ss, recv_sem=rs, device_id=dev, device_id_type=MESH)

    part = S // parts
    for i in range(parts):
        pltpu.make_async_copy(blocks_hbm.at[pl.ds(i * part, part)], blocks.at[pl.ds(i * part, part)],
                              blk_sem.at[i]).start()
    for ref in (cg0, cg1):
        ref[...] = jnp.zeros(ref.shape, bf16)
    runs[0] = jnp.zeros((slips, width), f32)

    barrier = pltpu.get_barrier_semaphore()

    def hello(dev):
        pl.semaphore_signal(barrier, inc=1, device_id=dev, device_id_type=MESH)

    @pl.when(z > 0)
    def _():
        hello((a, b - B))

    @pl.when(z < A - 1)
    def _():
        hello((a, b + B))

    for j in range(1, B):
        hello((a, z * B + (x + j) % B))
    for j in range(1, R):
        hello((((y + j) % R) * 2 + c, b))
    hello((y * 2 + 1 - c, b))
    ends = jnp.where(z > 0, 1, 0) + jnp.where(z < A - 1, 1, 0)
    pl.semaphore_wait(barrier, ends + (B - 1) + (R - 1) + 1)

    def product(t, source, out):
        mine = source[...]
        rg, cg = ((rg0, cg0), (rg1, cg1))[t]
        rg[b] = mine
        cg[a] = mine
        partner = (y * 2 + 1 - c, b)

        def z_copy(zi, up, k):
            idx = zi * B + x
            return rcopy(rg.at[idx], rg.at[idx], z_ss.at[t, up, k], rg_rs.at[t, idx],
                         (a, b + B if up else b - B))

        def x_copy(zi, j, side, k):
            idx = zi * B + x
            return rcopy(rg.at[idx], rg.at[idx], x_ss.at[t, side, k, j - 1], rg_rs.at[t, idx],
                         (a, z * B + (x + j) % B))

        def z_cases(k):
            lo, hi = z - k, z + k
            return ((1, lo, lo >= 0, z < A - 1), (0, hi, hi < A, z > 0))

        def gather_step(k):
            for up, zi, valid, onward in z_cases(k):
                @pl.when(valid)
                def _(up=up, zi=zi, onward=onward):
                    if k > 0:
                        idx = zi * B + x
                        rcopy(rg.at[idx], rg.at[idx], z_ss.at[t, up, k], rg_rs.at[t, idx],
                              partner).wait_recv()
                    if k < A - 1:
                        @pl.when(onward)
                        def _():
                            z_copy(zi, up, k).start()
                    if k > 0 or up:
                        for j in range(1, B):
                            x_copy(zi, j, up, k).start()

        def gather_sent():
            for k in range(A):
                for up, zi, valid, onward in z_cases(k):
                    @pl.when(valid)
                    def _(up=up, zi=zi, onward=onward):
                        if k < A - 1:
                            @pl.when(onward)
                            def _():
                                z_copy(zi, up, k).wait_send()
                        if k > 0 or up:
                            for j in range(1, B):
                                x_copy(zi, j, up, k).wait_send()

        def y_copy(j):
            return rcopy(cg.at[a], cg.at[a], cgy_ss.at[t, j], cg_rs.at[t, a], (j * 2 + c, b))

        def c_copy(yi):
            idx = yi * 2 + c
            return rcopy(cg.at[idx], cg.at[idx], cgc_ss.at[t, yi], cg_rs.at[t, idx], partner)

        def cg_wait(idx):
            rcopy(cg.at[idx], cg.at[idx], cgc_ss.at[t, 0], cg_rs.at[t, idx], partner).wait_recv()

        gather_step(0)
        for j in range(R):
            @pl.when(j < y)
            def _(j=j):
                y_copy(j).start()
        for j in range(R):
            @pl.when(j == y)
            def _(j=j):
                c_copy(j).start()
        for j in range(R):
            @pl.when(j > y)
            def _(j=j):
                cg_wait(j * 2 + c)
                c_copy(j).start()
        if t == 0:
            for i in range(parts):
                pltpu.make_async_copy(blocks_hbm.at[pl.ds(i * part, part)],
                                      blocks.at[pl.ds(i * part, part)], blk_sem.at[i]).wait()
        gather_step(1)
        for j in range(R):
            @pl.when(j >= y)
            def _(j=j):
                cg_wait(j * 2 + 1 - c)

        def near(first, last, group, base, transposed):
            @pl.loop(first, last)
            def _(k):
                s = plan[base, k]
                keep = plan[base + 2, k].astype(f32)
                v = group[plan[base + 1, k]]
                if transposed:
                    term = lax.dot_general(v, blocks[s], TRANS_B, preferred_element_type=f32)
                else:
                    term = jnp.dot(v, blocks[s], preferred_element_type=f32)
                runs[k + 1] = runs[k] * keep + term

        def far(group, n, here, there, first, second, base, m, out_ref):
            w = first.shape[1]

            def gather_coef(i, coef):
                pair = group[pl.ds(2 * i, 2)].reshape(2 * slips, width)
                got = jnp.dot(pair, first[...], preferred_element_type=f32)
                coef = jnp.where(here == 2 * i, got[:slips], coef)
                return jnp.where(here == 2 * i + 1, got[slips:], coef)

            coef = lax.fori_loop(0, n // 2, gather_coef, jnp.zeros((slips, w), f32))

            @pl.loop(0, m // 2)
            def _(i):
                both = jnp.concatenate([jnp.where(there == 2 * i, coef, 0.0),
                                        jnp.where(there == 2 * i + 1, coef, 0.0)], axis=0).astype(bf16)
                terms = lax.dot_general(both, second[...], TRANS_B, preferred_element_type=f32)
                out_ref[t, 2 * i] = (terms[:slips] + runs[plan[base + 3, 2 * i]]).astype(bf16)
                out_ref[t, 2 * i + 1] = (terms[slips:] + runs[plan[base + 3, 2 * i + 1]]).astype(bf16)

        cuts = [S * i // (A - 1) for i in range(A)]
        for k in range(A - 1):
            near(cuts[k], cuts[k + 1], cg, 0, True)
            if k + 2 < A:
                gather_step(k + 2)
        row_lane = planes[0:1, :]
        col_lane = planes[1:2, :]
        far(cg, NR, col_lane, row_lane, rcat, lcat, 0, NC, rp)

        def xr_copy(zi, j):
            to = (x + j) % B
            return rcopy(rp.at[t, zi * B + to], xr.at[t, j - 1, zi], xr_ss.at[t, j - 1, zi],
                         xr_rs.at[t, j - 1, zi], (a, z * B + to))

        def targets(d):
            return ((1, z + d, z + d < A), (0, z - d, z - d >= 0))

        for d in range(A - 1, -1, -1):
            for up, zi, valid in targets(d):
                if d > 0 or up:
                    @pl.when(valid)
                    def _(zi=zi):
                        for j in range(1, B):
                            xr_copy(zi, j).start()

        for j in range(1, B):
            for zi in range(A):
                idx = zi * B + (x + j) % B
                rcopy(rg.at[idx], rg.at[idx], x_ss.at[t, 0, 0, 0], rg_rs.at[t, idx], partner).wait_recv()

        def zr_copy(zi, up):
            return rcopy(zs.at[t, zi], zr.at[t, up, zi], zr_ss.at[t, zi], zr_rs.at[t, up, zi],
                         (a, b + B if up else b - B))

        def x_sum(zi):
            total = rp[t, zi * B + x].astype(f32)
            for j in range(1, B):
                xr_copy(zi, j).wait_recv()
                total += xr[t, j - 1, zi].astype(f32)
            return total

        def reduce_step(d):
            for up, zi, valid in targets(d):
                @pl.when(valid)
                def _(up=up, zi=zi):
                    zs[t, zi] = x_sum(zi).astype(bf16)

                    @pl.when(z > 0 if up else z < A - 1)
                    def _():
                        zr_copy(zi, up).wait_recv()
                        zs[t, zi] = (zs[t, zi].astype(f32) + zr[t, up, zi].astype(f32)).astype(bf16)

                    zr_copy(zi, up).start()

        cuts = [S * i // A for i in range(A + 1)]
        near(cuts[0], cuts[1], rg, 4, False)
        for k in range(1, A):
            near(cuts[k], cuts[k + 1], rg, 4, False)
            if k > 1:
                reduce_step(A + 1 - k)
        far(rg, NC, row_lane, col_lane, lcat, rcat, 4, NR, cp)

        def cr_copy(yi):
            return rcopy(cp.at[t, yi * 2 + 1 - c], cr.at[t, yi], cr_ss.at[t, yi], cr_rs.at[t, yi], partner)

        def yr_copy(yi):
            return rcopy(ys.at[t, yi], yr.at[t, y], yr_ss.at[t, yi], yr_rs.at[t, y], (yi * 2 + c, b))

        for j in range(R):
            @pl.when(j >= y)
            def _(j=j):
                cr_copy(j).start()
        for j in range(R):
            @pl.when(j > y)
            def _(j=j):
                cr_copy(j).wait_recv()
                ys[t, j] = (cp[t, j * 2 + c].astype(f32) + cr[t, j].astype(f32)).astype(bf16)
                yr_copy(j).start()
        reduce_step(1)
        cr_copy(y).wait_recv()
        runs[1] = cp[t, y * 2 + c].astype(f32) + cr[t, y].astype(f32)
        for j in range(R):
            @pl.when(j < y)
            def _(j=j):
                rcopy(ys.at[t, j], yr.at[t, j], yr_ss.at[t, j], yr_rs.at[t, j], partner).wait_recv()
                runs[1] = runs[1] + yr[t, j].astype(f32)
        runs[1] = runs[1] + x_sum(z)
        for up in (1, 0):
            @pl.when(z > 0 if up else z < A - 1)
            def _(up=up):
                zr_copy(z, up).wait_recv()
                runs[1] = runs[1] + zr[t, up, z].astype(f32)
        out[...] = runs[1].astype(bf16)

        def sent():
            gather_sent()
            for j in range(R):
                @pl.when(j < y)
                def _(j=j):
                    y_copy(j).wait_send()

                @pl.when(j >= y)
                def _(j=j):
                    c_copy(j).wait_send()
                    cr_copy(j).wait_send()

                @pl.when(j > y)
                def _(j=j):
                    yr_copy(j).wait_send()
            for zi in range(A):
                for j in range(1, B):
                    xr_copy(zi, j).wait_send()

                @pl.when(zi != z)
                def _(zi=zi):
                    zr_copy(zi, 0).wait_send()

        return sent

    first_sent = product(0, field, traction)
    second_sent = product(1, traction, response)
    first_sent()
    second_sent()


def run_plan(own, other, live, slots, outs, width):
    key = jnp.where(jnp.arange(slots) < live, own, outs)
    ids = jnp.arange(slots, dtype=jnp.int32)
    before = (key[None, :] < key[:, None]) | ((key[None, :] == key[:, None]) & (ids[None, :] < ids[:, None]))
    rank = jnp.sum(before.astype(jnp.int32), axis=1)
    hot = (rank[None, :] == ids[:, None]).astype(jnp.int32)
    order = jnp.sum(hot * ids[None, :], axis=1)
    load = jnp.sum(hot * other[None, :], axis=1)
    same = (key[None, :] == key[:, None]) & (ids[None, :] != ids[:, None]) & (rank[None, :] < rank[:, None])
    keep = jnp.sum(hot * jnp.any(same, axis=1).astype(jnp.int32)[None, :], axis=1)
    marks = jnp.arange(width, dtype=jnp.int32)
    upto = jnp.sum((key[None, :] <= marks[:, None]).astype(jnp.int32), axis=1)
    has = jnp.any(key[None, :] == marks[:, None], axis=1) & (marks < outs)
    last = jnp.where(has, upto, 0)
    pad = lambda v: jnp.pad(v, (0, width - v.shape[0]))
    return [pad(order), pad(load), pad(keep), last]


def shards(slip, near_pairs, near_blocks, near_live, far_pairs, far_left, far_right):
    NR, NC = lax.axis_size("row"), lax.axis_size("col")
    A = 4 if NC % 4 == 0 else 2
    B, R = NC // A, NR // 2
    slips = slip.shape[1]
    width = slip.shape[2] * slip.shape[3]
    S = near_pairs.shape[0]
    FS, rank = far_pairs.shape[0], far_left.shape[2]
    parts = 4 if S % 4 == 0 else 1
    pw = max(S, NC, NR)
    p, q = near_pairs[:, 0], near_pairs[:, 1]
    plan = jnp.stack(run_plan(p, q, near_live[0], S, NC, pw) + run_plan(q, p, near_live[0], S, NR, pw))
    planes = jnp.repeat(far_pairs.T, rank, axis=1)
    lcat = far_left.transpose(1, 0, 2).reshape(width, FS * rank)
    rcat = far_right.transpose(1, 0, 2).reshape(width, FS * rank)
    field = slip.reshape(slips, width)
    bf16 = jnp.bfloat16
    buf = lambda *lead: pltpu.VMEM(lead + (slips, width), bf16)
    dma = lambda *shape: pltpu.SemaphoreType.DMA(shape)
    x_others = max(B - 1, 1)
    vmem = pl.BlockSpec(memory_space=pltpu.VMEM)
    traction, response = pl.pallas_call(
        functools.partial(both_products, (A, B, R, S, parts)),
        out_shape=(jax.ShapeDtypeStruct((slips, width), bf16),) * 2,
        in_specs=[pl.BlockSpec(memory_space=pltpu.SMEM), vmem, vmem, vmem, vmem,
                  pl.BlockSpec(memory_space=pl.ANY)],
        out_specs=(vmem, vmem),
        scratch_shapes=[
            pltpu.VMEM((S, width, width), bf16),
            buf(NC), buf(NC), buf(NR), buf(NR), buf(2, NC), buf(2, x_others, A), buf(2, 2, A), buf(2, A),
            buf(2, NR), buf(2, R), buf(2, R), buf(2, R),
            pltpu.VMEM((S + 1, slips, width), jnp.float32),
            dma(parts), dma(2, NC), dma(2, NR), dma(2, 2, A), dma(2, 2, A, x_others), dma(2, R), dma(2, R),
            dma(2, x_others, A), dma(2, x_others, A), dma(2, A), dma(2, 2, A),
            dma(2, R), dma(2, R), dma(2, R), dma(2, R),
        ],
        compiler_params=pltpu.CompilerParams(
            collective_id=0, has_side_effects=True, vmem_limit_bytes=60 * 1024 * 1024),
    )(plan, field, planes, lcat, rcat, near_blocks)
    return traction.reshape(slip.shape), response.reshape(slip.shape)


def solution(mesh):
    in_specs = (
        P(("row", "col"), None, None, None),
        P(("row", "col"), None),
        P(("row", "col"), None, None),
        P(("row", "col")),
        P(("row", "col"), None),
        P(("row", "col"), None, None),
        P(("row", "col"), None, None),
    )
    out_specs = (P(("row", "col"), None, None, None), P(("row", "col"), None, None, None))
    return jax.shard_map(shards, mesh=mesh, in_specs=in_specs, out_specs=out_specs, check_vma=False)
```

profile of v0, /device:TPU:1, one launch (start us, length us, event | category | flops | bytes accessed | tf_op | source)
XLA Modules:
  0.0 114.2 jit_solution(12272009812105670304)
XLA Ops:
  1.3 0.8 compare_select_fusion.2
  2.0 0.8 slice_bitcast_fusion.1
  2.8 0.2 convert_reduce_fusion
  3.0 0.2 fusion.5
  3.2 0.2 fusion.4
  3.4 0.1 select_reduce_fusion.3
  3.6 0.1 select_reduce_fusion
  3.7 0.6 stack.29.plan
  4.3 0.7 broadcast_in_dim.28
  5.1 0.7 reshape.101.planes
  5.8 1.1 copy.22
  6.9 0.8 copy.23.field
  7.7 2.3 %copy.24.lcat = bf16[768,512]{1,0:T(8,128)(2,1)} copy(bf16[768,512]{0,1:T(8,128)(2,1)} %bitcast.43) | data formatting | bytes 1572864 | tf_op jit(solution)/shard_map/reshape | solution.py:330
  10.0 2.3 %copy.25.rcat = bf16[768,512]{1,0:T(8,128)(2,1)} copy(bf16[768,512]{0,1:T(8,128)(2,1)} %bitcast.44) | data formatting | bytes 1572864 | tf_op jit(solution)/shard_map/reshape | solution.py:331
  12.3 98.1 %shard_map.86 = (bf16[128,768]{1,0:T(8,128)(2,1)}, bf16[128,768]{1,0:T(8,128)(2,1)}) custom-call(s32[8,16]{1,0:T(8,128)} %stack.29.plan, bf16[128,768]{1,0:T(8,128)(2,1)} %copy.23.field, s32[2,512]{1,0:T(2,128)} %reshape.101.planes, bf16[768,512]{1,0:T(8,128)(2,1)} %copy.24.lcat, bf16[768,512]{1,0:T(8,128)(2,1)} %copy.25.rcat, bf16[16,768,768]{2,1,0:T(8,128)(2,1)} %blocks_hbm.1), custom_call_target="tpu_custom_call" | custom-call | tf_op jit(solution)/shard_map/pallas_call | solution.py:338
  110.4 1.1 copy.26
  111.5 0.8 copy.28
  112.3 1.1 copy.27
  113.4 0.8 copy.29
  (4 shorter events, 0.0 us)
where the time goes:
time: 115 us; the launch traced here: 114 us
  Pallas kernels  98.1 us (85%)
  local copies, waits for them, and re-layouts  12.4 us (11%)
  other arithmetic  2.4 us (2%)
  between operations  1.34 us (1%)
    pallas_call x1, Pallas kernels, shards(): pl.pallas_call(functools.partial(both_products, (A, B, R, S, parts)), out...  98.1 us
    unnamed x3, local copies, waits for them, and re-layouts  2.75 us
    reshape x1, local copies, waits for them, and re-layouts, shards(): rcat = far_right.transpose(1, 0, 2).reshape(width, FS * rank)  2.32 us

commit v1 on v0

--- a/solution.py
+++ b/solution.py
@@ -7,6 +7,7 @@
 from jax.experimental.pallas import tpu as pltpu
 from jax.sharding import PartitionSpec as P
 
+HALVES = 4
 MESH = pl.DeviceIdType.MESH
 TRANS_B = (((1,), (1,)), ((), ()))
 
@@ -15,7 +16,7 @@
                   blocks, rg0, rg1, cg0, cg1, rp, xr, zr, zs, cp, cr, yr, ys, runs,
                   blk_sem, rg_rs, cg_rs, z_ss, x_ss, cgy_ss, cgc_ss,
                   xr_ss, xr_rs, zr_ss, zr_rs, cr_ss, cr_rs, yr_ss, yr_rs):
-    A, B, R, S, parts = dims
+    A, B, R, S, parts, H = dims
     NC, NR = A * B, 2 * R
     slips, width = field.shape
     a, b = lax.axis_index("row"), lax.axis_index("col")
@@ -26,6 +27,11 @@
     def rcopy(src, dst, ss, rs, dev):
         return pltpu.make_async_remote_copy(
             src_ref=src, dst_ref=dst, send_sem=ss, recv_sem=rs, device_id=dev, device_id_type=MESH)
+
+    hr = slips // H
+
+    def rows(h):
+        return pl.ds(h * hr, hr)
 
     part = S // parts
     for i in range(parts):
@@ -63,48 +69,51 @@
         cg[a] = mine
         partner = (y * 2 + 1 - c, b)
 
-        def z_copy(zi, up, k):
+        def z_copy(zi, up, k, h):
             idx = zi * B + x
-            return rcopy(rg.at[idx], rg.at[idx], z_ss.at[t, up, k], rg_rs.at[t, idx],
+            return rcopy(rg.at[idx, rows(h)], rg.at[idx, rows(h)], z_ss.at[t, up, k, h], rg_rs.at[t, idx, h],
                          (a, b + B if up else b - B))
 
-        def x_copy(zi, j, side, k):
+        def x_copy(zi, j, side, k, h):
             idx = zi * B + x
-            return rcopy(rg.at[idx], rg.at[idx], x_ss.at[t, side, k, j - 1], rg_rs.at[t, idx],
-                         (a, z * B + (x + j) % B))
+            return rcopy(rg.at[idx, rows(h)], rg.at[idx, rows(h)], x_ss.at[t, side, k, h, j - 1],
+                         rg_rs.at[t, idx, h], (a, z * B + (x + j) % B))
+
+        def rg_wait(idx, h):
+            rcopy(rg.at[idx, rows(h)], rg.at[idx, rows(h)], x_ss.at[t, 0, 0, h, 0], rg_rs.at[t, idx, h],
+                  partner).wait_recv()
 
         def z_cases(k):
             lo, hi = z - k, z + k
             return ((1, lo, lo >= 0, z < A - 1), (0, hi, hi < A, z > 0))
 
-        def gather_step(k):
+        def gather_step(k, h):
             for up, zi, valid, onward in z_cases(k):
                 @pl.when(valid)
                 def _(up=up, zi=zi, onward=onward):
                     if k > 0:
-                        idx = zi * B + x
-                        rcopy(rg.at[idx], rg.at[idx], z_ss.at[t, up, k], rg_rs.at[t, idx],
-                              partner).wait_recv()
+                        rg_wait(zi * B + x, h)
                     if k < A - 1:
                         @pl.when(onward)
                         def _():
-                            z_copy(zi, up, k).start()
+                            z_copy(zi, up, k, h).start()
                     if k > 0 or up:
                         for j in range(1, B):
-                            x_copy(zi, j, up, k).start()
+                            x_copy(zi, j, up, k, h).start()
 
         def gather_sent():
             for k in range(A):
                 for up, zi, valid, onward in z_cases(k):
                     @pl.when(valid)
-                    def _(up=up, zi=zi, onward=onward):
-                        if k < A - 1:
-                            @pl.when(onward)
-                            def _():
-                                z_copy(zi, up, k).wait_send()
-                        if k > 0 or up:
-                            for j in range(1, B):
-                                x_copy(zi, j, up, k).wait_send()
+                    def _(k=k, up=up, zi=zi, onward=onward):
+                        for h in range(H):
+                            if k < A - 1:
+                                @pl.when(onward)
+                                def _(h=h):
+                                    z_copy(zi, up, k, h).wait_send()
+                            if k > 0 or up:
+                                for j in range(1, B):
+                                    x_copy(zi, j, up, k, h).wait_send()
 
         def y_copy(j):
             return rcopy(cg.at[a], cg.at[a], cgy_ss.at[t, j], cg_rs.at[t, a], (j * 2 + c, b))
@@ -116,7 +125,8 @@
         def cg_wait(idx):
             rcopy(cg.at[idx], cg.at[idx], cgc_ss.at[t, 0], cg_rs.at[t, idx], partner).wait_recv()
 
-        gather_step(0)
+        for h in range(H):
+            gather_step(0, h)
         for j in range(R):
             @pl.when(j < y)
             def _(j=j):
@@ -134,7 +144,8 @@
             for i in range(parts):
                 pltpu.make_async_copy(blocks_hbm.at[pl.ds(i * part, part)],
                                       blocks.at[pl.ds(i * part, part)], blk_sem.at[i]).wait()
-        gather_step(1)
+        for h in range(H):
+            gather_step(1, h)
         for j in range(R):
             @pl.when(j >= y)
             def _(j=j):
@@ -171,66 +182,75 @@
                 out_ref[t, 2 * i] = (terms[:slips] + runs[plan[base + 3, 2 * i]]).astype(bf16)
                 out_ref[t, 2 * i + 1] = (terms[slips:] + runs[plan[base + 3, 2 * i + 1]]).astype(bf16)
 
-        cuts = [S * i // (A - 1) for i in range(A)]
-        for k in range(A - 1):
-            near(cuts[k], cuts[k + 1], cg, 0, True)
-            if k + 2 < A:
-                gather_step(k + 2)
+        steps = [(k, h) for k in range(2, A) for h in range(H)]
+        n = len(steps) + 1
+        cuts = [S * i // n for i in range(n + 1)]
+        near(cuts[0], cuts[1], cg, 0, True)
+        for i, (k, h) in enumerate(steps):
+            gather_step(k, h)
+            near(cuts[i + 1], cuts[i + 2], cg, 0, True)
         row_lane = planes[0:1, :]
         col_lane = planes[1:2, :]
         far(cg, NR, col_lane, row_lane, rcat, lcat, 0, NC, rp)
 
-        def xr_copy(zi, j):
+        def xr_copy(zi, j, h):
             to = (x + j) % B
-            return rcopy(rp.at[t, zi * B + to], xr.at[t, j - 1, zi], xr_ss.at[t, j - 1, zi],
-                         xr_rs.at[t, j - 1, zi], (a, z * B + to))
+            return rcopy(rp.at[t, zi * B + to, rows(h)], xr.at[t, j - 1, zi, rows(h)], xr_ss.at[t, j - 1, zi, h],
+                         xr_rs.at[t, j - 1, zi, h], (a, z * B + to))
 
         def targets(d):
             return ((1, z + d, z + d < A), (0, z - d, z - d >= 0))
 
         for d in range(A - 1, -1, -1):
-            for up, zi, valid in targets(d):
-                if d > 0 or up:
-                    @pl.when(valid)
-                    def _(zi=zi):
-                        for j in range(1, B):
-                            xr_copy(zi, j).start()
+            for h in range(H):
+                for up, zi, valid in targets(d):
+                    if d > 0 or up:
+                        @pl.when(valid)
+                        def _(zi=zi, h=h):
+                            for j in range(1, B):
+                                xr_copy(zi, j, h).start()
 
         for j in range(1, B):
             for zi in range(A):
-                idx = zi * B + (x + j) % B
-                rcopy(rg.at[idx], rg.at[idx], x_ss.at[t, 0, 0, 0], rg_rs.at[t, idx], partner).wait_recv()
-
-        def zr_copy(zi, up):
-            return rcopy(zs.at[t, zi], zr.at[t, up, zi], zr_ss.at[t, zi], zr_rs.at[t, up, zi],
+                for h in range(H):
+                    rg_wait(zi * B + (x + j) % B, h)
+
+        def zr_copy(zi, up, h):
+            return rcopy(zs.at[t, zi, rows(h)], zr.at[t, up, zi, rows(h)], zr_ss.at[t, zi, h], zr_rs.at[t, up, zi, h],
                          (a, b + B if up else b - B))
 
-        def x_sum(zi):
-            total = rp[t, zi * B + x].astype(f32)
+        def x_sum(zi, h):
+            total = rp[t, zi * B + x, rows(h)].astype(f32)
             for j in range(1, B):
-                xr_copy(zi, j).wait_recv()
-                total += xr[t, j - 1, zi].astype(f32)
+                xr_copy(zi, j, h).wait_recv()
+                total += xr[t, j - 1, zi, rows(h)].astype(f32)
             return total
 
-        def reduce_step(d):
+        def reduce_step(d, h):
             for up, zi, valid in targets(d):
                 @pl.when(valid)
                 def _(up=up, zi=zi):
-                    zs[t, zi] = x_sum(zi).astype(bf16)
-
-                    @pl.when(z > 0 if up else z < A - 1)
+                    first = z == 0 if up else z == A - 1
+
+                    @pl.when(first)
                     def _():
-                        zr_copy(zi, up).wait_recv()
-                        zs[t, zi] = (zs[t, zi].astype(f32) + zr[t, up, zi].astype(f32)).astype(bf16)
-
-                    zr_copy(zi, up).start()
-
-        cuts = [S * i // A for i in range(A + 1)]
+                        zs[t, zi, rows(h)] = x_sum(zi, h).astype(bf16)
+
+                    @pl.when(jnp.logical_not(first))
+                    def _():
+                        total = x_sum(zi, h)
+                        zr_copy(zi, up, h).wait_recv()
+                        zs[t, zi, rows(h)] = (total + zr[t, up, zi, rows(h)].astype(f32)).astype(bf16)
+
+                    zr_copy(zi, up, h).start()
+
+        steps = [(d, h) for d in range(A - 1, 1, -1) for h in range(H)]
+        n = len(steps) + 1
+        cuts = [S * i // n for i in range(n + 1)]
         near(cuts[0], cuts[1], rg, 4, False)
-        for k in range(1, A):
-            near(cuts[k], cuts[k + 1], rg, 4, False)
-            if k > 1:
-                reduce_step(A + 1 - k)
+        for i, (d, h) in enumerate(steps):
+            reduce_step(d, h)
+            near(cuts[i + 1], cuts[i + 2], rg, 4, False)
         far(rg, NC, row_lane, col_lane, lcat, rcat, 4, NR, cp)
 
         def cr_copy(yi):
@@ -249,7 +269,8 @@
                 cr_copy(j).wait_recv()
                 ys[t, j] = (cp[t, j * 2 + c].astype(f32) + cr[t, j].astype(f32)).astype(bf16)
                 yr_copy(j).start()
-        reduce_step(1)
+        for h in range(H):
+            reduce_step(1, h)
         cr_copy(y).wait_recv()
         runs[1] = cp[t, y * 2 + c].astype(f32) + cr[t, y].astype(f32)
         for j in range(R):
@@ -257,13 +278,14 @@
             def _(j=j):
                 rcopy(ys.at[t, j], yr.at[t, j], yr_ss.at[t, j], yr_rs.at[t, j], partner).wait_recv()
                 runs[1] = runs[1] + yr[t, j].astype(f32)
-        runs[1] = runs[1] + x_sum(z)
-        for up in (1, 0):
-            @pl.when(z > 0 if up else z < A - 1)
-            def _(up=up):
-                zr_copy(z, up).wait_recv()
-                runs[1] = runs[1] + zr[t, up, z].astype(f32)
-        out[...] = runs[1].astype(bf16)
+        for h in range(H):
+            runs[1, rows(h)] = runs[1, rows(h)] + x_sum(z, h)
+            for up in (1, 0):
+                @pl.when(z > 0 if up else z < A - 1)
+                def _(up=up, h=h):
+                    zr_copy(z, up, h).wait_recv()
+                    runs[1, rows(h)] = runs[1, rows(h)] + zr[t, up, z, rows(h)].astype(f32)
+            out[rows(h)] = runs[1, rows(h)].astype(bf16)
 
         def sent():
             gather_sent()
@@ -281,12 +303,13 @@
                 def _(j=j):
                     yr_copy(j).wait_send()
             for zi in range(A):
-                for j in range(1, B):
-                    xr_copy(zi, j).wait_send()
-
-                @pl.when(zi != z)
-                def _(zi=zi):
-                    zr_copy(zi, 0).wait_send()
+                for h in range(H):
+                    for j in range(1, B):
+                        xr_copy(zi, j, h).wait_send()
+
+                    @pl.when(zi != z)
+                    def _(zi=zi, h=h):
+                        zr_copy(zi, 0, h).wait_send()
 
         return sent
 
@@ -323,6 +346,7 @@
     S = near_pairs.shape[0]
     FS, rank = far_pairs.shape[0], far_left.shape[2]
     parts = 4 if S % 4 == 0 else 1
+    H = HALVES if slips % (16 * HALVES) == 0 else 1
     pw = max(S, NC, NR)
     p, q = near_pairs[:, 0], near_pairs[:, 1]
     plan = jnp.stack(run_plan(p, q, near_live[0], S, NC, pw) + run_plan(q, p, near_live[0], S, NR, pw))
@@ -336,7 +360,7 @@
     x_others = max(B - 1, 1)
     vmem = pl.BlockSpec(memory_space=pltpu.VMEM)
     traction, response = pl.pallas_call(
-        functools.partial(both_products, (A, B, R, S, parts)),
+        functools.partial(both_products, (A, B, R, S, parts, H)),
         out_shape=(jax.ShapeDtypeStruct((slips, width), bf16),) * 2,
         in_specs=[pl.BlockSpec(memory_space=pltpu.SMEM), vmem, vmem, vmem, vmem,
                   pl.BlockSpec(memory_space=pl.ANY)],
@@ -346,8 +370,8 @@
             buf(NC), buf(NC), buf(NR), buf(NR), buf(2, NC), buf(2, x_others, A), buf(2, 2, A), buf(2, A),
             buf(2, NR), buf(2, R), buf(2, R), buf(2, R),
             pltpu.VMEM((S + 1, slips, width), jnp.float32),
-            dma(parts), dma(2, NC), dma(2, NR), dma(2, 2, A), dma(2, 2, A, x_others), dma(2, R), dma(2, R),
-            dma(2, x_others, A), dma(2, x_others, A), dma(2, A), dma(2, 2, A),
+            dma(parts), dma(2, NC, H), dma(2, NR), dma(2, 2, A, H), dma(2, 2, A, H, x_others), dma(2, R), dma(2, R),
+            dma(2, x_others, A, H), dma(2, x_others, A, H), dma(2, A, H), dma(2, 2, A, H),
             dma(2, R), dma(2, R), dma(2, R), dma(2, R),
         ],
         compiler_params=pltpu.CompilerParams(

time: 115 us -> 107 us (0.930)
  Pallas kernels: 98.1 us -> 90.2 us
    pallas_call x1, Pallas kernels: 98.1 us -> 90.2 us  [shards(): pl.pallas_call(functools.partial(both_products, (A, B, R, S, parts, H)),...]
where the time goes in v1:
time: 107 us; the launch traced here: 106 us
  Pallas kernels  90.2 us (84%)
  local copies, waits for them, and re-layouts  12.4 us (12%)
  other arithmetic  2.4 us (2%)
  between operations  1.34 us (1%)
    pallas_call x1, Pallas kernels, shards(): pl.pallas_call(functools.partial(both_products, (A, B, R, S, parts, H)),...  90.2 us
    unnamed x3, local copies, waits for them, and re-layouts  2.75 us
    reshape x1, local copies, waits for them, and re-layouts, shards(): rcat = far_right.transpose(1, 0, 2).reshape(width, FS * rank)  2.32 us
    reshape x1, local copies, waits for them, and re-layouts, shards(): lcat = far_left.transpose(1, 0, 2).reshape(width, FS * rank)  2.29 us
    pallas_call x2, local copies, waits for them, and re-layouts, shards(): pl.pallas_call(functools.partial(both_products, (A, B, R, S, parts, H)),...  2.17 us

profile of v1, /device:TPU:1, one launch (start us, length us, event | category | flops | bytes accessed | tf_op | source)
XLA Modules:
  0.0 106.3 jit_solution(10003089777918167485)
XLA Ops:
  1.3 0.8 compare_select_fusion.2
  2.0 0.8 slice_bitcast_fusion.1
  2.8 0.2 convert_reduce_fusion
  3.0 0.2 fusion.5
  3.2 0.2 fusion.4
  3.4 0.1 select_reduce_fusion.3
  3.6 0.1 select_reduce_fusion
  3.7 0.6 stack.29.plan
  4.3 0.7 broadcast_in_dim.28
  5.1 0.7 reshape.101.planes
  5.8 1.1 %copy.22 = bf16[1,128,3,256]{1,3,2,0:T(8,128)(2,1)S(1)} copy(bf16[1,128,3,256]{3,1,2,0:T(8,128)(2,1)} %param.7) | data formatting | bytes 393216 | tf_op args[0]
  6.9 0.8 copy.23.field
  7.7 2.3 %copy.24.lcat = bf16[768,512]{1,0:T(8,128)(2,1)} copy(bf16[768,512]{0,1:T(8,128)(2,1)} %bitcast.43) | data formatting | bytes 1572864 | tf_op jit(solution)/shard_map/reshape | solution.py:354
  10.0 2.3 %copy.25.rcat = bf16[768,512]{1,0:T(8,128)(2,1)} copy(bf16[768,512]{0,1:T(8,128)(2,1)} %bitcast.44) | data formatting | bytes 1572864 | tf_op jit(solution)/shard_map/reshape | solution.py:355
  12.3 90.2 %shard_map.86 = (bf16[128,768]{1,0:T(8,128)(2,1)}, bf16[128,768]{1,0:T(8,128)(2,1)}) custom-call(s32[8,16]{1,0:T(8,128)} %stack.29.plan, bf16[128,768]{1,0:T(8,128)(2,1)} %copy.23.field, s32[2,512]{1,0:T(2,128)} %reshape.101.planes, bf16[768,512]{1,0:T(8,128)(2,1)} %copy.24.lcat, bf16[768,512]{1,0:T(8,128)(2,1)} %copy.25.rcat, bf16[16,768,768]{2,1,0:T(8,128)(2,1)} %blocks_hbm.1), custom_call_target="tpu_custom_call" | custom-call | tf_op jit(solution)/shard_map/pallas_call | solution.py:362
  102.5 1.1 %copy.26 = bf16[128,768]{0,1:T(8,128)(2,1)S(1)} copy(bf16[128,768]{1,0:T(8,128)(2,1)} %get-tuple-element.4) | data formatting | bytes 393216 | tf_op jit(solution)/shard_map/pallas_call | solution.py:362
  103.6 0.8 copy.28
  104.4 1.1 %copy.27 = bf16[128,768]{0,1:T(8,128)(2,1)S(1)} copy(bf16[128,768]{1,0:T(8,128)(2,1)} %get-tuple-element.5) | data formatting | bytes 393216 | tf_op jit(solution)/shard_map/pallas_call | solution.py:362
  105.5 0.8 copy.29
  (4 shorter events, 0.0 us)
